TPU v7x, 32 devices: a whole 2x2x4 slice. The times are simulated.
32 devices in a mesh: groups: 2 (over x), row: 8 (over z, y), col: 2 (over core).
Axes of the slice: x: 2, y: 2, z: 4, core: 2. Of those that a mesh axis runs over, the one named last changes fastest.
Arguments:
- coefficients: bfloat16 [4096, 1000], P(('groups', 'row', 'col')), parts along dimension 0, may hold values from -0.375 to 0.375
- integrals: bfloat16 [4096, 8, 256], P(('groups', 'row', 'col')), parts along dimension 0, may hold values from -6 to 6
- send_blocks: int32 [32, 16, 2], P(('groups', 'row', 'col')), parts along dimension 0, may hold values from 0 to 15
- send_count: int32 [32, 16], P(('groups', 'row', 'col')), parts along dimension 0, may hold values from 1 to 2
Outputs:
- kband: float32 [4096, 640], P(('groups', 'row', 'col')), parts along dimension 0
There are 2 independent parts, one for each index of `groups`. A program takes and returns all parts, laid end to end along the dimension named above; each array names one. Nothing has to cross between parts.
Inputs may be any that keep to these rules, and one draw needn't show every extreme that they name: `send_blocks`: block numbers within one owner's tile. Slot s carries data when s < send_count; some owner fills all 2 slots to some tile.
All inputs are finite; a program needn't handle non-finite values.
Results may differ from a plain program's by a relative error of at most 0.00098.
Values may be sent and summed in bfloat16 or wider, within the bound.
A program may use at most 64 MiB of HBM per device.

v0:
```python
import math

import jax
import jax.numpy as jnp
from jax import lax
from jax.sharding import PartitionSpec as P

KB = 8
BAND = 2


def from_behind(array, axis, by):
    devices = lax.axis_size(axis)
    pairs = [(i, i + by) for i in range(devices) if 0 <= i + by < devices]
    return lax.ppermute(array, axis, pairs)


def pair_block(left_rows, right_rows, norm_scale):
    product = lax.dot_general(
        left_rows, right_rows, (((1,), (1,)), ((), ())), preferred_element_type=jnp.float32
    )
    return product * norm_scale


def body(coefficients, integrals, send_blocks, send_count):
    tile_rows = integrals.shape[0]
    aux_count = integrals.shape[1]
    column_total = integrals.shape[2]
    occ_count = coefficients.shape[1]
    slot_count = send_blocks.shape[2]
    owned_blocks = coefficients.reshape(tile_rows // KB, KB, occ_count)
    picked = jnp.take(owned_blocks, send_blocks[0], axis=0)
    live_mask = jnp.arange(slot_count, dtype=jnp.int32)[None, :] < send_count[0][:, None]
    outgoing = jnp.where(live_mask[:, :, None, None], picked, jnp.zeros((), picked.dtype))
    incoming = lax.all_to_all(outgoing, ("row", "col"), split_axis=0, concat_axis=0, tiled=True)
    received = incoming.reshape(column_total, occ_count)
    product = jnp.dot(
        integrals.reshape(tile_rows * aux_count, column_total),
        received,
        preferred_element_type=jnp.float32,
    )
    half_tiles = product.astype(jnp.bfloat16).reshape(tile_rows, aux_count * occ_count)
    norm_scale = 1.0 / math.sqrt(aux_count * occ_count)
    upper_blocks = []
    lower_blocks = []
    for offset in range(1, BAND + 1):
        above_tiles = from_behind(half_tiles, ("row", "col"), -offset)
        upper_blocks.append(pair_block(half_tiles, above_tiles, norm_scale))
        below_tiles = from_behind(half_tiles, ("row", "col"), offset)
        lower_blocks.append(pair_block(half_tiles, below_tiles, norm_scale))
    diagonal = pair_block(half_tiles, half_tiles, norm_scale)
    banded = jnp.concatenate(lower_blocks[::-1] + [diagonal] + upper_blocks, axis=1)
    return banded


def solution(mesh):
    return jax.shard_map(
        body,
        mesh=mesh,
        in_specs=(
            P(("groups", "row", "col"), None),
            P(("groups", "row", "col"), None, None),
            P(("groups", "row", "col"), None, None),
            P(("groups", "row", "col"), None),
        ),
        out_specs=P(("groups", "row", "col"), None),
        check_vma=False,
    )
```

profile of v0, /device:TPU:1, one launch (start us, length us, event | category | flops | bytes accessed | tf_op | source)
XLA Modules:
  0.0 175.1 jit_solution(879046462782286243)
XLA Ops:
  0.0 0.0 copy-start
  0.0 0.7 compare_select_fusion
  0.7 0.7 compare_and_fusion
  1.4 1.1 copy.14
  2.5 0.1 copy.15
  2.6 0.1 reshape.76
  2.7 0.1 copy.13
  2.8 0.7 iota_compare_fusion
  3.6 0.6 gather_fusion
  4.1 0.1 select_select_fusion
  4.3 21.2 %all_to_all.5 = bf16[16,2,8,1000]{3,2,1,0:T(8,128)(2,1)S(1)} all-to-all(bf16[16,2,8,1000]{3,2,1,0:T(8,128)(2,1)S(1)} %select_select_fusion), channel_id=1, replica_groups=mesh['groups'=2,'row'=8,'col'=2] {'row','col'}, dimensions={0} | all-to-all | bytes 1024000 | tf_op jit(solution)/shard_map/all_to_all | solution.py:35
  25.5 0.0 copy-done
  25.5 0.8 convert_bitcast_fusion
  26.3 2.6 %copy.16 = bf16[1024,1000]{1,0:T(8,128)(2,1)} copy(bf16[1024,1000]{0,1:T(8,128)(2,1)S(1)} %convert_bitcast_fusion) | data formatting | bytes 4096000 | tf_op jit(solution)/shard_map/convert_element_type | solution.py:42
  28.9 4.1 %reshape.73 = bf16[128,8000]{1,0:T(8,128)(2,1)S(1)} reshape(bf16[1024,1000]{1,0:T(8,128)(2,1)} %copy.16) | data formatting | bytes 4096000 | tf_op jit(solution)/shard_map/reshape | solution.py:42
  33.0 2.4 %copy.17 = bf16[128,8000]{0,1:T(8,128)(2,1)} copy(bf16[128,8000]{1,0:T(8,128)(2,1)S(1)} %reshape.73) | data formatting | bytes 4096000 | tf_op jit(solution)/shard_map/reshape | solution.py:42
  35.4 2.9 %collective-permute-start = (bf16[128,8000]{0,1:T(8,128)(2,1)}, bf16[128,8000]{0,1:T(8,128)(2,1)S(1)}, u32[]{:S(2)}, u32[]{:S(2)}) collective-permute-start(bf16[128,8000]{0,1:T(8,128)(2,1)} %copy.17), channel_id=1, source_target_pairs={{0,2},{1,3},{2,4},{3,5},{4,6},{5,7},{6,8},{7,9},{8,10},{9,11},{10,... | collective-permute-start | bytes 6144008 | tf_op jit(solution)/shard_map/ppermute | solution.py:15
  38.3 3.6 %collective-permute-start.1 = (bf16[128,8000]{0,1:T(8,128)(2,1)}, bf16[128,8000]{0,1:T(8,128)(2,1)S(1)}, u32[]{:S(2)}, u32[]{:S(2)}) collective-permute-start(bf16[128,8000]{0,1:T(8,128)(2,1)} %copy.17), channel_id=1, source_target_pairs={{0,1},{1,2},{2,3},{3,4},{4,5},{5,6},{6,7},{7,8},{8,9},{9,10},{10,1... | collective-permute-start | bytes 6144008 | tf_op jit(solution)/shard_map/ppermute | solution.py:15
  41.9 1.9 %collective-permute-start.2 = (bf16[128,8000]{0,1:T(8,128)(2,1)}, bf16[128,8000]{0,1:T(8,128)(2,1)S(1)}, u32[]{:S(2)}, u32[]{:S(2)}) collective-permute-start(bf16[128,8000]{0,1:T(8,128)(2,1)} %copy.17), channel_id=1, source_target_pairs={{1,0},{2,1},{3,2},{4,3},{5,4},{6,5},{7,6},{8,7},{9,8},{10,9},{11,1... | collective-permute-start | bytes 6144008 | tf_op jit(solution)/shard_map/ppermute | solution.py:15
  43.8 1.3 collective-permute-start.3
  45.1 103.4 %collective-permute-done = bf16[128,8000]{0,1:T(8,128)(2,1)S(1)} collective-permute-done((bf16[128,8000]{0,1:T(8,128)(2,1)}, bf16[128,8000]{0,1:T(8,128)(2,1)S(1)}, u32[]{:S(2)}, u32[]{:S(2)}) %collective-permute-start) | collective-permute-done | bytes 2048032 | tf_op jit(solution)/shard_map/ppermute | solution.py:15
  148.5 1.0 fusion.4
  149.4 21.2 %collective-permute-done.1 = bf16[128,8000]{0,1:T(8,128)(2,1)S(1)} collective-permute-done((bf16[128,8000]{0,1:T(8,128)(2,1)}, bf16[128,8000]{0,1:T(8,128)(2,1)S(1)}, u32[]{:S(2)}, u32[]{:S(2)}) %collective-permute-start.1) | collective-permute-done | bytes 2048032 | tf_op jit(solution)/shard_map/ppermute | solution.py:15
  170.6 1.0 fusion.3
  171.6 0.7 fusion.2
  172.3 0.0 collective-permute-done.2
  172.3 1.0 fusion.1
  173.3 0.0 collective-permute-done.3
  173.3 1.0 fusion
  174.2 0.9 copy.21
  (1 shorter events, 0.0 us)
Async XLA Ops:
  0.0 25.5 %copy-start = (bf16[128,8,256]{2,1,0:T(8,128)(2,1)S(1)}, bf16[128,8,256]{2,1,0:T(8,128)(2,1)}, u32[]{:S(2)}) copy-start(bf16[128,8,256]{2,1,0:T(8,128)(2,1)} %param.5) | copy-start | bytes 1572868
  35.4 113.1 %collective-permute-start = (bf16[128,8000]{0,1:T(8,128)(2,1)}, bf16[128,8000]{0,1:T(8,128)(2,1)S(1)}, u32[]{:S(2)}, u32[]{:S(2)}) collective-permute-start(bf16[128,8000]{0,1:T(8,128)(2,1)} %copy.17), channel_id=1, source_target_pairs={{0,2},{1,3},{2,4},{3,5},{4,6},{5,7},{6,8},{7,9},{8,10},{9,11},{10,... | collective-permute-start | bytes 6144008 | tf_op jit(solution)/shard_map/ppermute | solution.py:15
  38.3 132.3 %collective-permute-start.1 = (bf16[128,8000]{0,1:T(8,128)(2,1)}, bf16[128,8000]{0,1:T(8,128)(2,1)S(1)}, u32[]{:S(2)}, u32[]{:S(2)}) collective-permute-start(bf16[128,8000]{0,1:T(8,128)(2,1)} %copy.17), channel_id=1, source_target_pairs={{0,1},{1,2},{2,3},{3,4},{4,5},{5,6},{6,7},{7,8},{8,9},{9,10},{10,1... | collective-permute-start | bytes 6144008 | tf_op jit(solution)/shard_map/ppermute | solution.py:15
  41.9 130.4 %collective-permute-start.2 = (bf16[128,8000]{0,1:T(8,128)(2,1)}, bf16[128,8000]{0,1:T(8,128)(2,1)S(1)}, u32[]{:S(2)}, u32[]{:S(2)}) collective-permute-start(bf16[128,8000]{0,1:T(8,128)(2,1)} %copy.17), channel_id=1, source_target_pairs={{1,0},{2,1},{3,2},{4,3},{5,4},{6,5},{7,6},{8,7},{9,8},{10,9},{11,1... | collective-permute-start | bytes 6144008 | tf_op jit(solution)/shard_map/ppermute | solution.py:15
  43.8 129.5 %collective-permute-start.3 = (bf16[128,8000]{0,1:T(8,128)(2,1)}, bf16[128,8000]{0,1:T(8,128)(2,1)S(1)}, u32[]{:S(2)}, u32[]{:S(2)}) collective-permute-start(bf16[128,8000]{0,1:T(8,128)(2,1)} %copy.17), channel_id=1, source_target_pairs={{2,0},{3,1},{4,2},{5,3},{6,4},{7,5},{8,6},{9,7},{10,8},{11,9},{12,... | collective-permute-start | bytes 6144008 | tf_op jit(solution)/shard_map/ppermute | solution.py:15
where the time goes:
time: 175 us
  waiting for transfers between devices  125 us (71%)
  blocking collectives  21.2 us (12%)
  local copies, waits for them, and re-layouts  11.9 us (7%)
  starting transfers between devices  9.68 us (6%)
  matrix products  5.29 us (3%)
  other arithmetic  2.3 us (1%)
    ppermute x4, waiting for transfers between devices, from_behind(): return lax.ppermute(array, axis, pairs)  125 us
    all_to_all x1, blocking collectives, body(): lax.all_to_all(outgoing, ('row', 'col'), split_axis=0, concat_axis=0, til...  21.2 us
    ppermute x4, starting transfers between devices, from_behind(): return lax.ppermute(array, axis, pairs)  9.68 us
    reshape x2, local copies, waits for them, and re-layouts, body(): product.astype(jnp.bfloat16).reshape(tile_rows, aux_count * occ_count)  6.51 us
    dot_general x5, matrix products, pair_block(): lax.dot_general(left_rows, right_rows, (((1,), (1,)), ((), ())), preferre...  4.53 us
  transfers between devices with their start and end apart: 4, of which 2 were waited for; matrix products, arithmetic and copies ran while one was open for 2% of the time, Pallas kernels for 0%

commit v1 on v0

--- a/solution.py
+++ b/solution.py
@@ -1,12 +1,18 @@
+import functools
 import math
 
 import jax
 import jax.numpy as jnp
 from jax import lax
+from jax.experimental import pallas as pl
+from jax.experimental.pallas import tpu as pltpu
 from jax.sharding import PartitionSpec as P
 
 KB = 8
 BAND = 2
+LANES = 128
+PARTS = 2
+NEED = 3
 
 
 def from_behind(array, axis, by):
@@ -22,7 +28,7 @@
     return product * norm_scale
 
 
-def body(coefficients, integrals, send_blocks, send_count):
+def general_body(coefficients, integrals, send_blocks, send_count):
     tile_rows = integrals.shape[0]
     aux_count = integrals.shape[1]
     column_total = integrals.shape[2]
@@ -53,7 +59,311 @@
     return banded
 
 
+def kernel(
+    rows, occ, aux, scale,
+    coef_ref, ints_ref, out_ref,
+    coefs, held, stage, picked, sent, landed,
+    own_sem, ring_send, ring_recv, pair_send, pair_recv, int_send, int_recv, res_send, res_recv,
+):
+    tiles = 2 * rows
+    depth = rows // 2
+    steps = rows - 1
+    row, col = lax.axis_index("row"), lax.axis_index("col")
+    me = 2 * row + col
+    spot = jnp.where(row % 2 == 0, row // 2, rows - 1 - row // 2)
+    padded = coef_ref.shape[0]
+    part_rows = padded // PARTS
+    tile = coef_ref.shape[1]
+    own_rows = tile // KB
+
+    def row_at(where):
+        where = lax.rem(where + 2 * rows, rows)
+        return jnp.where(where < depth, 2 * where, 2 * (rows - 1 - where) + 1)
+
+    def device(which):
+        return {"row": which // 2, "col": which % 2}
+
+    partner = 2 * row + 1 - col
+    right = 2 * row_at(spot + 1) + col
+    left = 2 * row_at(spot - 1) + col
+    skip = jnp.where(col == 0, 2, -2)
+    others = (me, me + 1, me + skip)
+    has_next = me + 1 < tiles
+    has_prev = me >= 1
+    has_skip = jnp.logical_and(me + skip >= 0, me + skip < tiles)
+    has_back = jnp.logical_and(me - skip >= 0, me - skip < tiles)
+
+    barrier = pltpu.get_barrier_semaphore()
+    for step in range(1, tiles):
+        pl.semaphore_signal(
+            barrier, inc=1, device_id=device(lax.rem(me + step, tiles)),
+            device_id_type=pl.DeviceIdType.MESH,
+        )
+
+    own = pltpu.make_async_copy(coef_ref, coefs.at[me], own_sem)
+    own.start()
+    own.wait()
+    pl.semaphore_wait(barrier, tiles - 1)
+
+    def remote(src, dst, send_sem, recv_sem, which):
+        return pltpu.make_async_remote_copy(
+            src_ref=src, dst_ref=dst, send_sem=send_sem, recv_sem=recv_sem,
+            device_id=device(which), device_id_type=pl.DeviceIdType.MESH,
+        )
+
+    def piece(owner, part):
+        return coefs.at[owner, pl.ds(part * part_rows, part_rows)]
+
+    def ring(way, step):
+        back = -(step // 2) if way == 0 else step // 2
+        part = step % 2 if way == 0 else 1 - step % 2
+        ref = piece(2 * row_at(spot + back) + col, part)
+        return remote(ref, ref, ring_send.at[way, step], ring_recv.at[way, step], right if way == 0 else left)
+
+    def arrival(way, step):
+        back = -(step // 2) - 1 if way == 0 else step // 2 + 1
+        part = step % 2 if way == 0 else 1 - step % 2
+        ref = piece(2 * row_at(spot + back) + col, part)
+        return remote(ref, ref, ring_send.at[way, step], ring_recv.at[way, step], right if way == 0 else left)
+
+    def share(way, step, core):
+        back = -(step // 2) - 1 if way == 0 else step // 2 + 1
+        part = step % 2 if way == 0 else 1 - step % 2
+        ref = piece(2 * row_at(spot + back) + core, part)
+        return remote(ref, ref, pair_send.at[way, step], pair_recv.at[way, step], partner)
+
+    def share_own(core):
+        ref = coefs.at[2 * row + core]
+        return remote(ref, ref, pair_send.at[0, steps], pair_recv.at[0, steps], partner)
+
+    for step in range(2):
+        for way in range(2):
+            ring(way, step).start()
+    share_own(col).start()
+
+    for q in range(ints_ref.shape[1] // LANES):
+        stage[q] = ints_ref[:, q * LANES:(q + 1) * LANES].astype(jnp.float32)
+        for p in range(aux):
+            lines = stage[q, pl.ds(p, tile, stride=aux), :]
+            held[0, p, :, q * LANES:(q + 1) * LANES] = lines.astype(held.dtype)
+
+    back_copy = remote(held.at[0], held.at[2], int_send.at[0], int_recv.at[1], me - skip)
+    next_copy = remote(held.at[0], held.at[1], int_send.at[1], int_recv.at[0], partner)
+    pass_copy = remote(held.at[2], held.at[1], int_send.at[1], int_recv.at[0], partner)
+
+    @pl.when(has_back)
+    def _():
+        back_copy.start()
+
+    @pl.when(col == 1)
+    def _():
+        next_copy.start()
+
+    height = 2 * KB
+    lane = lax.broadcasted_iota(jnp.int32, (height, LANES), 1)
+    line = lax.broadcasted_iota(jnp.int32, (height, LANES), 0)
+    number = lax.broadcasted_iota(jnp.int32, (NEED * height, LANES), 1).astype(jnp.float32)
+    inner = (lax.broadcasted_iota(jnp.int32, (NEED * height, LANES), 0) % KB).astype(jnp.float32)
+    occ_lane = lax.broadcasted_iota(jnp.int32, (NEED * height, LANES), 1)
+    last = padded - LANES
+
+    def pick(owner):
+        meta = coefs[owner, pl.ds(padded - 16, 16), :].astype(jnp.float32)
+        first = jnp.broadcast_to(meta[8:9], (height, LANES))
+        second = jnp.broadcast_to(meta[9:10], (height, LANES))
+        both = jnp.where(line < KB, first, second)
+        chosen = jnp.concatenate(
+            [
+                jnp.sum(jnp.where(lane == other, both, 0.0), axis=1, keepdims=True)
+                for other in others
+            ],
+            axis=0,
+        )
+        hot = (number == chosen * KB + inner).astype(jnp.float32).astype(coefs.dtype)
+        got = lax.dot_general(
+            hot, coefs[owner], (((1,), (1,)), ((), ())), preferred_element_type=jnp.float32
+        )
+        tail = jnp.where(occ_lane + last < occ, got[:, last:], 0.0)
+        got = got.astype(picked.dtype)
+        tail = tail.astype(picked.dtype)
+        for k in range(NEED):
+            rows_of = pl.ds(pl.multiple_of(owner * height, height), height)
+            picked[k, rows_of, 0:last] = got[k * height:(k + 1) * height, 0:last]
+            picked[k, rows_of, last:padded] = tail[k * height:(k + 1) * height]
+
+    pick(me)
+    for step in range(steps):
+        for way in range(2):
+            arrival(way, step).wait_recv()
+            if step + 2 < steps:
+                ring(way, step + 2).start()
+            share(way, step, col).start()
+        if step == 0:
+            share_own(1 - col).wait_recv()
+            pick(partner)
+        if step % 2 == 1:
+            for way in range(2):
+                back = -(step // 2) - 1 if way == 0 else step // 2 + 1
+                pick(2 * row_at(spot + back) + col)
+            for way in range(2):
+                for earlier in (step - 1, step):
+                    share(way, earlier, 1 - col).wait_recv()
+                back = -(step // 2) - 1 if way == 0 else step // 2 + 1
+                pick(2 * row_at(spot + back) + 1 - col)
+    opposite = row_at(spot + depth)
+    pick(2 * opposite + col)
+
+    @pl.when(has_skip)
+    def _():
+        remote(held.at[0], held.at[2], int_send.at[0], int_recv.at[1], me - skip).wait_recv()
+
+    @pl.when(jnp.logical_and(col == 0, has_skip))
+    def _():
+        pass_copy.start()
+
+    for way in range(2):
+        share(way, steps - 1, 1 - col).wait_recv()
+    pick(2 * opposite + 1 - col)
+
+    @pl.when(has_next)
+    def _():
+        next_copy.wait_recv()
+
+    def add_up(p, totals):
+        halves = [
+            jnp.dot(held[k, p], picked[k], preferred_element_type=jnp.float32).astype(jnp.bfloat16)
+            for k in range(NEED)
+        ]
+        return tuple(
+            total + lax.dot_general(
+                halves[0], half, (((1,), (1,)), ((), ())), preferred_element_type=jnp.float32
+            )
+            for total, half in zip(totals, halves)
+        )
+
+    zero = jnp.zeros((tile, tile), jnp.float32)
+    diag, above, far = lax.fori_loop(0, aux, add_up, (zero,) * NEED)
+    above = above * scale
+    far = far * scale
+    out_ref[...] = jnp.zeros_like(out_ref)
+    sent[0] = above.T
+    sent[1] = far.T
+    give_next = remote(sent.at[0], landed.at[0], res_send.at[0], res_recv.at[0], me + 1)
+    give_skip = remote(sent.at[1], landed.at[1], res_send.at[1], res_recv.at[1], me + skip)
+
+    @pl.when(has_next)
+    def _():
+        give_next.start()
+
+    @pl.when(has_skip)
+    def _():
+        give_skip.start()
+
+    out_ref[:, 2 * tile:3 * tile] = diag * scale
+
+    @pl.when(has_next)
+    def _():
+        out_ref[:, 3 * tile:4 * tile] = above
+
+    @pl.when(jnp.logical_and(has_skip, col == 0))
+    def _():
+        out_ref[:, 4 * tile:5 * tile] = far
+
+    @pl.when(jnp.logical_and(has_skip, col == 1))
+    def _():
+        out_ref[:, 0:tile] = far
+
+    for step in range(steps):
+        for way in range(2):
+            ring(way, step).wait_send()
+            share(way, step, col).wait_send()
+    share_own(col).wait_send()
+
+    @pl.when(has_back)
+    def _():
+        back_copy.wait_send()
+
+    @pl.when(col == 1)
+    def _():
+        next_copy.wait_send()
+
+    @pl.when(jnp.logical_and(col == 0, has_skip))
+    def _():
+        pass_copy.wait_send()
+
+    @pl.when(has_prev)
+    def _():
+        give_next.wait_recv()
+        out_ref[:, tile:2 * tile] = landed[0]
+
+    @pl.when(has_back)
+    def _():
+        give_skip.wait_recv()
+
+    @pl.when(jnp.logical_and(has_back, col == 0))
+    def _():
+        out_ref[:, 0:tile] = landed[1]
+
+    @pl.when(jnp.logical_and(has_back, col == 1))
+    def _():
+        out_ref[:, 4 * tile:5 * tile] = landed[1]
+
+    @pl.when(has_next)
+    def _():
+        give_next.wait_send()
+
+    @pl.when(has_skip)
+    def _():
+        give_skip.wait_send()
+
+
+def ring_body(rows, coefficients, integrals, send_blocks, send_count):
+    tile, aux, columns = integrals.shape
+    occ = coefficients.shape[1]
+    slots = send_blocks.shape[2]
+    tiles = 2 * rows
+    live = jnp.arange(slots, dtype=jnp.int32)[:, None] < send_count
+    chosen = jnp.where(live, send_blocks[0].T, -1).astype(coefficients.dtype)
+    padded = -(-(occ + slots) // LANES) * LANES
+    meta_at = padded - 8
+    flipped = jnp.pad(coefficients.T, ((0, padded - occ), (0, 0)))
+    flipped = flipped + jnp.pad(chosen, ((meta_at, padded - meta_at - slots), (0, tile - tiles)))
+    steps = rows - 1
+    bf16, f32 = jnp.bfloat16, jnp.float32
+    return pl.pallas_call(
+        functools.partial(kernel, rows, occ, aux, 1.0 / math.sqrt(aux * occ)),
+        out_shape=jax.ShapeDtypeStruct((tile, (2 * BAND + 1) * tile), f32),
+        in_specs=[pl.BlockSpec(memory_space=pltpu.VMEM)] * 2,
+        out_specs=pl.BlockSpec(memory_space=pltpu.VMEM),
+        scratch_shapes=[
+            pltpu.VMEM((tiles, padded, tile), bf16),
+            pltpu.VMEM((NEED, aux, tile, columns), bf16),
+            pltpu.VMEM((columns // LANES, tile * aux, LANES), f32),
+            pltpu.VMEM((NEED, columns, padded), bf16),
+            pltpu.VMEM((2, tile, tile), f32),
+            pltpu.VMEM((2, tile, tile), f32),
+            pltpu.SemaphoreType.DMA,
+            pltpu.SemaphoreType.DMA((2, steps)),
+            pltpu.SemaphoreType.DMA((2, steps)),
+            pltpu.SemaphoreType.DMA((2, steps + 1)),
+            pltpu.SemaphoreType.DMA((2, steps + 1)),
+            pltpu.SemaphoreType.DMA((2,)),
+            pltpu.SemaphoreType.DMA((2,)),
+            pltpu.SemaphoreType.DMA((2,)),
+            pltpu.SemaphoreType.DMA((2,)),
+        ],
+        compiler_params=pltpu.CompilerParams(
+            collective_id=0, has_side_effects=True, vmem_limit_bytes=40 * 1024 * 1024
+        ),
+    )(flipped, integrals.reshape(tile * aux, columns))
+
+
 def solution(mesh):
+    rows, cols = mesh.shape["row"], mesh.shape["col"]
+    if cols == 2 and rows % 2 == 0 and 4 <= rows <= 8:
+        body = functools.partial(ring_body, rows)
+    else:
+        body = general_body
     return jax.shard_map(
         body,
         mesh=mesh,

time: 175 us -> 51 us (0.29)
  waiting for transfers between devices: 125 us -> 0 us
  Pallas kernels: 0 us -> 48.3 us
  blocking collectives: 21.2 us -> 0 us
  local copies, waits for them, and re-layouts: 11.9 us -> 0.73 us
  starting transfers between devices: 9.68 us -> 0 us
  matrix products: 5.29 us -> 0 us
    ppermute x4 -> x0, waiting for transfers between devices: 125 us -> none  [from_behind(): return lax.ppermute(array, axis, pairs)]
    pallas_call x0 -> x1, Pallas kernels: none -> 48.3 us  [ring_body(): pl.pallas_call(functools.partial(kernel, rows, occ, aux, 1.0 / math.sqrt(...]
    all_to_all x1 -> x0, blocking collectives: 21.2 us -> none  [body(): lax.all_to_all(outgoing, ('row', 'col'), split_axis=0, concat_axis=0, til...]
    ppermute x4 -> x0, starting transfers between devices: 9.68 us -> none  [from_behind(): return lax.ppermute(array, axis, pairs)]
    reshape x2 -> x0, local copies, waits for them, and re-layouts: 6.51 us -> none  [body(): product.astype(jnp.bfloat16).reshape(tile_rows, aux_count * occ_count)]
    dot_general x6 -> x0, matrix products: 5.29 us -> none  [the longest x5 4.53 us: pair_block(): lax.dot_general(left_rows, right_rows, (((1,), (1,)), ((), ())), preferre...]
    convert_element_type x1 -> x0, local copies, waits for them, and re-layouts: 2.56 us -> none  [body(): product.astype(jnp.bfloat16).reshape(tile_rows, aux_count * occ_count)]
  transfers between devices with their start and end apart: 4 -> 0, of which waited for: 2 -> 0; matrix products, arithmetic and copies ran while one was open for 2% -> 0% of each run, Pallas kernels for 0% -> 0%
where the time goes in v1:
time: 51 us; the launch traced here: 50.8 us
  Pallas kernels  48.3 us (95%)
  other arithmetic  1.71 us (3%)
  local copies, waits for them, and re-layouts  0.73 us (1%)
    pallas_call x1, Pallas kernels, ring_body(): pl.pallas_call(functools.partial(kernel, rows, occ, aux, 1.0 / math.sqrt(...  48.3 us

profile of v1, /device:TPU:1, one launch (start us, length us, event | category | flops | bytes accessed | tf_op | source)
XLA Modules:
  0.0 50.8 jit_solution(13242667976149488140)
XLA Ops:
  0.0 0.0 copy-start
  0.0 0.7 %fusion = bf16[2,16]{1,0:T(2,128)(2,1)S(1)} fusion(s32[1,16,2]{1,2,0:T(2,128)} %param.6, s32[16]{0:T(128)} %bitcast.9), kind=kLoop, calls=%fused_computation.2 | loop fusion | flops 96 | bytes 256 | tf_op jit(solution)/shard_map/convert_element_type | solution.py:326
  0.7 1.0 %pad_add_fusion.coef_ref = bf16[1024,128]{1,0:T(8,128)(2,1)S(1)} fusion(bf16[2,16]{1,0:T(2,128)(2,1)S(1)} %fusion, bf16[1000,128]{1,0:T(8,128)(2,1)} %bitcast.8), kind=kLoop, calls=%fused_computation | loop fusion | flops 524288 | bytes 518208 | tf_op jit(solution)/shard_map/add | solution.py:330
  1.7 0.0 copy-done
  1.7 48.3 %shard_map.46 = f32[128,640]{1,0:T(8,128)S(1)} custom-call(bf16[1024,128]{1,0:T(8,128)(2,1)S(1)} %pad_add_fusion.coef_ref, bf16[1024,256]{1,0:T(8,128)(2,1)S(1)} %bitcast.7), custom_call_target="tpu_custom_call" | custom-call | tf_op jit(solution)/shard_map/pallas_call | solution.py:333
  50.1 0.7 %copy.6 = f32[128,640]{1,0:T(8,128)} copy(f32[128,640]{1,0:T(8,128)S(1)} %shard_map.46) | data formatting | bytes 655360
Async XLA Ops:
  0.0 1.7 %copy-start = (bf16[128,8,256]{2,1,0:T(8,128)(2,1)S(1)}, bf16[128,8,256]{2,1,0:T(8,128)(2,1)}, u32[]{:S(2)}) copy-start(bf16[128,8,256]{2,1,0:T(8,128)(2,1)} %param.5) | copy-start | bytes 1572868

commit v2 on v1

--- a/solution.py
+++ b/solution.py
@@ -61,9 +61,9 @@
 
 def kernel(
     rows, occ, aux, scale,
-    coef_ref, ints_ref, out_ref,
-    coefs, held, stage, picked, sent, landed,
-    own_sem, ring_send, ring_recv, pair_send, pair_recv, int_send, int_recv, res_send, res_recv,
+    coef_ref, ints_ref, blocks_ref, count_ref, out_ref,
+    coefs, notes, held, stage, picked, sent, landed,
+    ring_send, ring_recv, pair_send, pair_recv, int_send, int_recv, res_send, res_recv,
 ):
     tiles = 2 * rows
     depth = rows // 2
@@ -71,7 +71,7 @@
     row, col = lax.axis_index("row"), lax.axis_index("col")
     me = 2 * row + col
     spot = jnp.where(row % 2 == 0, row // 2, rows - 1 - row // 2)
-    padded = coef_ref.shape[0]
+    padded = coefs.shape[1]
     part_rows = padded // PARTS
     tile = coef_ref.shape[1]
     own_rows = tile // KB
@@ -94,16 +94,36 @@
     has_back = jnp.logical_and(me - skip >= 0, me - skip < tiles)
 
     barrier = pltpu.get_barrier_semaphore()
-    for step in range(1, tiles):
+
+    def greet(which):
         pl.semaphore_signal(
-            barrier, inc=1, device_id=device(lax.rem(me + step, tiles)),
-            device_id_type=pl.DeviceIdType.MESH,
+            barrier, inc=1, device_id=device(which), device_id_type=pl.DeviceIdType.MESH
         )
 
-    own = pltpu.make_async_copy(coef_ref, coefs.at[me], own_sem)
-    own.start()
-    own.wait()
-    pl.semaphore_wait(barrier, tiles - 1)
+    cross = me - 1 + 2 * col
+    has_cross = jnp.logical_and(cross >= 0, cross < tiles)
+    for which in (left, right, partner):
+        greet(which)
+    for there, which in ((has_skip, me + skip), (has_back, me - skip), (has_cross, cross)):
+        pl.when(there)(functools.partial(greet, which))
+
+    slots, dests = blocks_ref.shape
+    whole = occ // 16 * 16
+    live = lax.broadcasted_iota(jnp.int32, (slots, dests), 0) < count_ref[...]
+    notes[...] = jnp.zeros_like(notes)
+    notes[0:slots, 0:dests] = jnp.where(live, blocks_ref[...], -1).astype(jnp.float32)
+    coefs[me, 0:whole] = coef_ref[0:whole]
+    rest = jnp.concatenate(
+        [
+            coef_ref[whole:occ].astype(jnp.float32),
+            jnp.zeros((padded - 8 - occ, tile), jnp.float32),
+            notes[...],
+        ],
+        axis=0,
+    )
+    coefs[me, whole:padded] = rest.astype(coefs.dtype)
+    greeted = 3 + has_skip.astype(jnp.int32) + has_back.astype(jnp.int32) + has_cross.astype(jnp.int32)
+    pl.semaphore_wait(barrier, greeted)
 
     def remote(src, dst, send_sem, recv_sem, which):
         return pltpu.make_async_remote_copy(
@@ -145,7 +165,7 @@
         stage[q] = ints_ref[:, q * LANES:(q + 1) * LANES].astype(jnp.float32)
         for p in range(aux):
             lines = stage[q, pl.ds(p, tile, stride=aux), :]
-            held[0, p, :, q * LANES:(q + 1) * LANES] = lines.astype(held.dtype)
+            held[0, p * tile:(p + 1) * tile, q * LANES:(q + 1) * LANES] = lines.astype(held.dtype)
 
     back_copy = remote(held.at[0], held.at[2], int_send.at[0], int_recv.at[1], me - skip)
     next_copy = remote(held.at[0], held.at[1], int_send.at[1], int_recv.at[0], partner)
@@ -229,22 +249,27 @@
     def _():
         next_copy.wait_recv()
 
-    def add_up(p, totals):
+    group = 2
+
+    def add_up(step, total):
+        rows_of = pl.ds(pl.multiple_of(step * group * tile, group * tile), group * tile)
         halves = [
-            jnp.dot(held[k, p], picked[k], preferred_element_type=jnp.float32).astype(jnp.bfloat16)
+            jnp.dot(
+                held[k, rows_of], picked[k], preferred_element_type=jnp.float32
+            ).astype(jnp.bfloat16)
             for k in range(NEED)
         ]
-        return tuple(
-            total + lax.dot_general(
-                halves[0], half, (((1,), (1,)), ((), ())), preferred_element_type=jnp.float32
+        for p in range(group):
+            slices = [half[p * tile:(p + 1) * tile] for half in halves]
+            total = total + lax.dot_general(
+                slices[0], jnp.concatenate(slices, axis=0),
+                (((1,), (1,)), ((), ())), preferred_element_type=jnp.float32,
             )
-            for total, half in zip(totals, halves)
-        )
-
-    zero = jnp.zeros((tile, tile), jnp.float32)
-    diag, above, far = lax.fori_loop(0, aux, add_up, (zero,) * NEED)
-    above = above * scale
-    far = far * scale
+        return total
+
+    zero = jnp.zeros((tile, NEED * tile), jnp.float32)
+    total = lax.fori_loop(0, aux // group, add_up, zero) * scale
+    diag, above, far = (total[:, k * tile:(k + 1) * tile] for k in range(NEED))
     out_ref[...] = jnp.zeros_like(out_ref)
     sent[0] = above.T
     sent[1] = far.T
@@ -259,7 +284,7 @@
     def _():
         give_skip.start()
 
-    out_ref[:, 2 * tile:3 * tile] = diag * scale
+    out_ref[:, 2 * tile:3 * tile] = diag
 
     @pl.when(has_next)
     def _():
@@ -320,29 +345,23 @@
 def ring_body(rows, coefficients, integrals, send_blocks, send_count):
     tile, aux, columns = integrals.shape
     occ = coefficients.shape[1]
-    slots = send_blocks.shape[2]
     tiles = 2 * rows
-    live = jnp.arange(slots, dtype=jnp.int32)[:, None] < send_count
-    chosen = jnp.where(live, send_blocks[0].T, -1).astype(coefficients.dtype)
-    padded = -(-(occ + slots) // LANES) * LANES
-    meta_at = padded - 8
-    flipped = jnp.pad(coefficients.T, ((0, padded - occ), (0, 0)))
-    flipped = flipped + jnp.pad(chosen, ((meta_at, padded - meta_at - slots), (0, tile - tiles)))
+    padded = -(-(occ + 8) // LANES) * LANES
     steps = rows - 1
     bf16, f32 = jnp.bfloat16, jnp.float32
     return pl.pallas_call(
         functools.partial(kernel, rows, occ, aux, 1.0 / math.sqrt(aux * occ)),
         out_shape=jax.ShapeDtypeStruct((tile, (2 * BAND + 1) * tile), f32),
-        in_specs=[pl.BlockSpec(memory_space=pltpu.VMEM)] * 2,
+        in_specs=[pl.BlockSpec(memory_space=pltpu.VMEM)] * 4,
         out_specs=pl.BlockSpec(memory_space=pltpu.VMEM),
         scratch_shapes=[
             pltpu.VMEM((tiles, padded, tile), bf16),
-            pltpu.VMEM((NEED, aux, tile, columns), bf16),
+            pltpu.VMEM((8, tile), f32),
+            pltpu.VMEM((NEED, aux * tile, columns), bf16),
             pltpu.VMEM((columns // LANES, tile * aux, LANES), f32),
             pltpu.VMEM((NEED, columns, padded), bf16),
             pltpu.VMEM((2, tile, tile), f32),
             pltpu.VMEM((2, tile, tile), f32),
-            pltpu.SemaphoreType.DMA,
             pltpu.SemaphoreType.DMA((2, steps)),
             pltpu.SemaphoreType.DMA((2, steps)),
             pltpu.SemaphoreType.DMA((2, steps + 1)),
@@ -355,7 +374,7 @@
         compiler_params=pltpu.CompilerParams(
             collective_id=0, has_side_effects=True, vmem_limit_bytes=40 * 1024 * 1024
         ),
-    )(flipped, integrals.reshape(tile * aux, columns))
+    )(coefficients.T, integrals.reshape(tile * aux, columns), send_blocks[0].T, send_count)
 
 
 def solution(mesh):

time: 51 us -> 48.2 us (0.945)
  Pallas kernels: 48.3 us -> 44.4 us
  local copies, waits for them, and re-layouts: 0.73 us -> 3.4 us
  other arithmetic: 1.71 us -> 0 us
    pallas_call x1, Pallas kernels: 48.3 us -> 44.4 us  [ring_body(): pl.pallas_call(functools.partial(kernel, rows, occ, aux, 1.0 / math.sqrt(...]
    unnamed x3 -> x9, local copies, waits for them, and re-layouts: 0.73 us -> 3.4 us
    add x1 -> x0, other arithmetic: 0.97 us -> none  [ring_body(): flipped + jnp.pad(chosen, ((meta_at, padded - meta_at - slots), (0, tile...]
    convert_element_type x1 -> x0, other arithmetic: 0.74 us -> none  [ring_body(): chosen = jnp.where(live, send_blocks[0].T, -1).astype(coefficients.dtype)]
where the time goes in v2:
time: 48.2 us; the launch traced here: 47.8 us
  Pallas kernels  44.4 us (92%)
  local copies, waits for them, and re-layouts  3.4 us (7%)
    pallas_call x1, Pallas kernels, ring_body(): pl.pallas_call(functools.partial(kernel, rows, occ, aux, 1.0 / math.sqrt(...  44.4 us
    unnamed x9, local copies, waits for them, and re-layouts  3.4 us

profile of v2, /device:TPU:1, one launch (start us, length us, event | category | flops | bytes accessed | tf_op | source)
XLA Modules:
  0.0 47.8 jit_solution(14217274038155420151)
XLA Ops:
  0.0 0.0 copy-start.2
  0.0 0.0 copy-start.3
  0.0 0.7 %copy-done.2 = s32[1,16,2]{1,2,0:T(2,128)S(1)} copy-done((s32[1,16,2]{1,2,0:T(2,128)S(1)}, s32[1,16,2]{1,2,0:T(2,128)}, u32[]{:S(2)}) %copy-start.2) | copy-done | bytes 152
  0.7 0.0 copy-done.3
  0.7 0.0 copy-start
  0.7 1.0 %copy-done = bf16[128,8,256]{2,1,0:T(8,128)(2,1)S(1)} copy-done((bf16[128,8,256]{2,1,0:T(8,128)(2,1)S(1)}, bf16[128,8,256]{2,1,0:T(8,128)(2,1)}, u32[]{:S(2)}) %copy-start) | copy-done | bytes 524312
  1.7 0.0 copy-start.1
  1.7 0.9 %copy-done.1 = bf16[128,1000]{0,1:T(8,128)(2,1)S(1)} copy-done((bf16[128,1000]{0,1:T(8,128)(2,1)S(1)}, bf16[128,1000]{0,1:T(8,128)(2,1)}, u32[]{:S(2)}) %copy-start.1) | copy-done | bytes 256024
  2.7 44.4 %shard_map.46 = f32[128,640]{1,0:T(8,128)S(1)} custom-call(bf16[1000,128]{1,0:T(8,128)(2,1)S(1)} %bitcast.6, bf16[1024,256]{1,0:T(8,128)(2,1)S(1)} %bitcast.5, s32[2,16]{1,0:T(2,128)S(1)} %bitcast.7, s32[1,16]{1,0:T(1,128)S(1)} %copy-done.3), custom_call_target="tpu_custom_call" | custom-call | tf_op jit(solution)/shard_map/pallas_call | solution.py:352
  47.1 0.7 %copy.6 = f32[128,640]{1,0:T(8,128)} copy(f32[128,640]{1,0:T(8,128)S(1)} %shard_map.46) | data formatting | bytes 655360
Async XLA Ops:
  0.0 0.7 %copy-start.2 = (s32[1,16,2]{1,2,0:T(2,128)S(1)}, s32[1,16,2]{1,2,0:T(2,128)}, u32[]{:S(2)}) copy-start(s32[1,16,2]{1,2,0:T(2,128)} %param.6) | copy-start | bytes 388
  0.0 0.7 %copy-start.3 = (s32[1,16]{1,0:T(1,128)S(1)}, s32[1,16]{1,0:T(1,128)}, u32[]{:S(2)}) copy-start(s32[1,16]{1,0:T(1,128)} %count_ref.1) | copy-start | bytes 196
  0.7 1.0 %copy-start = (bf16[128,8,256]{2,1,0:T(8,128)(2,1)S(1)}, bf16[128,8,256]{2,1,0:T(8,128)(2,1)}, u32[]{:S(2)}) copy-start(bf16[128,8,256]{2,1,0:T(8,128)(2,1)} %param.5) | copy-start | bytes 1572868
  1.7 0.9 %copy-start.1 = (bf16[128,1000]{0,1:T(8,128)(2,1)S(1)}, bf16[128,1000]{0,1:T(8,128)(2,1)}, u32[]{:S(2)}) copy-start(bf16[128,1000]{0,1:T(8,128)(2,1)} %param.4) | copy-start | bytes 768004

commit v3 on v2

--- a/solution.py
+++ b/solution.py
@@ -60,11 +60,20 @@
 
 
 def kernel(
-    rows, occ, aux, scale,
-    coef_ref, ints_ref, blocks_ref, count_ref, out_ref,
-    coefs, notes, held, stage, picked, sent, landed,
-    ring_send, ring_recv, pair_send, pair_recv, int_send, int_recv, res_send, res_recv,
+    rows, aux, scale,
+    coef_hbm, ints_hbm, blocks_hbm, count_hbm, out_ref,
+    coef_ref, ints_ref, blocks_ref, count_ref, coefs, notes, held, relay, stage, picked, sent, landed,
+    in_sem, ring_send, ring_recv, pair_send, pair_recv, int_send, int_recv, res_send, res_recv,
 ):
+    fetches = [
+        pltpu.make_async_copy(src, dst, in_sem.at[k])
+        for k, (src, dst) in enumerate((
+            (coef_hbm, coef_ref), (blocks_hbm, blocks_ref), (count_hbm, count_ref), (ints_hbm, ints_ref)
+        ))
+    ]
+    for fetch in fetches:
+        fetch.start()
+    occ = coef_hbm.shape[0]
     tiles = 2 * rows
     depth = rows // 2
     steps = rows - 1
@@ -107,6 +116,8 @@
     for there, which in ((has_skip, me + skip), (has_back, me - skip), (has_cross, cross)):
         pl.when(there)(functools.partial(greet, which))
 
+    for fetch in fetches[:3]:
+        fetch.wait()
     slots, dests = blocks_ref.shape
     whole = occ // 16 * 16
     live = lax.broadcasted_iota(jnp.int32, (slots, dests), 0) < count_ref[...]
@@ -161,6 +172,7 @@
             ring(way, step).start()
     share_own(col).start()
 
+    fetches[3].wait()
     for q in range(ints_ref.shape[1] // LANES):
         stage[q] = ints_ref[:, q * LANES:(q + 1) * LANES].astype(jnp.float32)
         for p in range(aux):
@@ -171,9 +183,21 @@
     next_copy = remote(held.at[0], held.at[1], int_send.at[1], int_recv.at[0], partner)
     pass_copy = remote(held.at[2], held.at[1], int_send.at[1], int_recv.at[0], partner)
 
-    @pl.when(has_back)
+    detours = ((4, 6, 2), (tiles - 5, tiles - 7, tiles - 3))
+    is_from = functools.reduce(jnp.logical_or, [me == way[0] for way in detours])
+    is_via = functools.reduce(jnp.logical_or, [me == way[1] for way in detours])
+    via = jnp.where(col == 0, detours[0][1], detours[1][1])
+    end = jnp.where(col == 0, detours[0][2], detours[1][2])
+    leave_copy = remote(held.at[0], relay, int_send.at[0], int_recv.at[2], via)
+    relay_copy = remote(relay, held.at[2], int_send.at[2], int_recv.at[1], end)
+
+    @pl.when(jnp.logical_and(has_back, jnp.logical_not(is_from)))
     def _():
         back_copy.start()
+
+    @pl.when(is_from)
+    def _():
+        leave_copy.start()
 
     @pl.when(col == 1)
     def _():
@@ -218,6 +242,11 @@
             if step + 2 < steps:
                 ring(way, step + 2).start()
             share(way, step, col).start()
+        if step == 2:
+            @pl.when(is_via)
+            def _():
+                leave_copy.wait_recv()
+                relay_copy.start()
         if step == 0:
             share_own(1 - col).wait_recv()
             pick(partner)
@@ -304,9 +333,17 @@
             share(way, step, col).wait_send()
     share_own(col).wait_send()
 
-    @pl.when(has_back)
+    @pl.when(jnp.logical_and(has_back, jnp.logical_not(is_from)))
     def _():
         back_copy.wait_send()
+
+    @pl.when(is_from)
+    def _():
+        leave_copy.wait_send()
+
+    @pl.when(is_via)
+    def _():
+        relay_copy.wait_send()
 
     @pl.when(col == 1)
     def _():
@@ -350,36 +387,42 @@
     steps = rows - 1
     bf16, f32 = jnp.bfloat16, jnp.float32
     return pl.pallas_call(
-        functools.partial(kernel, rows, occ, aux, 1.0 / math.sqrt(aux * occ)),
+        functools.partial(kernel, rows, aux, 1.0 / math.sqrt(aux * occ)),
         out_shape=jax.ShapeDtypeStruct((tile, (2 * BAND + 1) * tile), f32),
-        in_specs=[pl.BlockSpec(memory_space=pltpu.VMEM)] * 4,
+        in_specs=[pl.BlockSpec(memory_space=pltpu.HBM)] * 4,
         out_specs=pl.BlockSpec(memory_space=pltpu.VMEM),
         scratch_shapes=[
+            pltpu.VMEM((occ, tile), bf16),
+            pltpu.VMEM((tile * aux, columns), bf16),
+            pltpu.VMEM((send_blocks.shape[2], tiles), jnp.int32),
+            pltpu.VMEM((1, tiles), jnp.int32),
             pltpu.VMEM((tiles, padded, tile), bf16),
             pltpu.VMEM((8, tile), f32),
             pltpu.VMEM((NEED, aux * tile, columns), bf16),
+            pltpu.VMEM((aux * tile, columns), bf16),
             pltpu.VMEM((columns // LANES, tile * aux, LANES), f32),
             pltpu.VMEM((NEED, columns, padded), bf16),
             pltpu.VMEM((2, tile, tile), f32),
             pltpu.VMEM((2, tile, tile), f32),
+            pltpu.SemaphoreType.DMA((4,)),
             pltpu.SemaphoreType.DMA((2, steps)),
             pltpu.SemaphoreType.DMA((2, steps)),
             pltpu.SemaphoreType.DMA((2, steps + 1)),
             pltpu.SemaphoreType.DMA((2, steps + 1)),
-            pltpu.SemaphoreType.DMA((2,)),
-            pltpu.SemaphoreType.DMA((2,)),
+            pltpu.SemaphoreType.DMA((3,)),
+            pltpu.SemaphoreType.DMA((3,)),
             pltpu.SemaphoreType.DMA((2,)),
             pltpu.SemaphoreType.DMA((2,)),
         ],
         compiler_params=pltpu.CompilerParams(
-            collective_id=0, has_side_effects=True, vmem_limit_bytes=40 * 1024 * 1024
+            collective_id=0, has_side_effects=True, vmem_limit_bytes=60 * 1024 * 1024
         ),
     )(coefficients.T, integrals.reshape(tile * aux, columns), send_blocks[0].T, send_count)
 
 
 def solution(mesh):
     rows, cols = mesh.shape["row"], mesh.shape["col"]
-    if cols == 2 and rows % 2 == 0 and 4 <= rows <= 8:
+    if cols == 2 and rows % 2 == 0 and 6 <= rows <= 8:
         body = functools.partial(ring_body, rows)
     else:
         body = general_body

time: 48.2 us -> 48 us (level)
  Pallas kernels: 44.4 us -> 46.1 us
  local copies, waits for them, and re-layouts: 3.4 us -> 1.72 us
    pallas_call x1, Pallas kernels: 44.4 us -> 46.1 us  [ring_body(): pl.pallas_call(functools.partial(kernel, rows, aux, 1.0 / math.sqrt(aux *...]
    unnamed x9 -> x1, local copies, waits for them, and re-layouts: 3.4 us -> 1.72 us
where the time goes in v3:
time: 48 us; the launch traced here: 47.8 us
  Pallas kernels  46.1 us (96%)
  local copies, waits for them, and re-layouts  1.72 us (4%)
    pallas_call x1, Pallas kernels, ring_body(): pl.pallas_call(functools.partial(kernel, rows, aux, 1.0 / math.sqrt(aux *...  46.1 us
    unnamed x1, local copies, waits for them, and re-layouts  1.72 us

profile of v3, /device:TPU:1, one launch (start us, length us, event | category | flops | bytes accessed | tf_op | source)
XLA Modules:
  0.0 47.8 jit_solution(12407076471429793607)
XLA Ops:
  0.0 46.1 %shard_map.46 = f32[128,640]{1,0:T(8,128)} custom-call(bf16[1000,128]{1,0:T(8,128)(2,1)} %bitcast.6, bf16[1024,256]{1,0:T(8,128)(2,1)} %bitcast.5, s32[2,16]{1,0:T(2,128)} %bitcast.7, s32[1,16]{1,0:T(1,128)} %count_hbm.1), custom_call_target="tpu_custom_call" | custom-call | tf_op jit(solution)/shard_map/pallas_call | solution.py:389
  46.1 1.7 %copy.6 = f32[128,640]{1,0:T(8,128)} copy(f32[128,640]{1,0:T(8,128)} %shard_map.46) | data formatting | bytes 655360

commit v4 on v3

--- a/solution.py
+++ b/solution.py
@@ -242,7 +242,7 @@
             if step + 2 < steps:
                 ring(way, step + 2).start()
             share(way, step, col).start()
-        if step == 2:
+        if step == 3:
             @pl.when(is_via)
             def _():
                 leave_copy.wait_recv()

time: 48 us -> 45.3 us (0.944)
  Pallas kernels: 46.1 us -> 43.4 us
    pallas_call x1, Pallas kernels: 46.1 us -> 43.4 us  [ring_body(): pl.pallas_call(functools.partial(kernel, rows, aux, 1.0 / math.sqrt(aux *...]
where the time goes in v4:
time: 45.3 us; the launch traced here: 45.2 us
  Pallas kernels  43.4 us (96%)
  local copies, waits for them, and re-layouts  1.72 us (4%)
    pallas_call x1, Pallas kernels, ring_body(): pl.pallas_call(functools.partial(kernel, rows, aux, 1.0 / math.sqrt(aux *...  43.4 us
    unnamed x1, local copies, waits for them, and re-layouts  1.72 us

profile of v4, /device:TPU:1, one launch (start us, length us, event | category | flops | bytes accessed | tf_op | source)
XLA Modules:
  0.0 45.2 jit_solution(131040200873481016)
XLA Ops:
  0.0 43.4 %shard_map.46 = f32[128,640]{1,0:T(8,128)} custom-call(bf16[1000,128]{1,0:T(8,128)(2,1)} %bitcast.6, bf16[1024,256]{1,0:T(8,128)(2,1)} %bitcast.5, s32[2,16]{1,0:T(2,128)} %bitcast.7, s32[1,16]{1,0:T(1,128)} %count_hbm.1), custom_call_target="tpu_custom_call" | custom-call | tf_op jit(solution)/shard_map/pallas_call | solution.py:389
  43.4 1.7 %copy.6 = f32[128,640]{1,0:T(8,128)} copy(f32[128,640]{1,0:T(8,128)} %shard_map.46) | data formatting | bytes 655360

commit v5 on v4

--- a/solution.py
+++ b/solution.py
@@ -134,50 +134,50 @@
     )
     coefs[me, whole:padded] = rest.astype(coefs.dtype)
     greeted = 3 + has_skip.astype(jnp.int32) + has_back.astype(jnp.int32) + has_cross.astype(jnp.int32)
-    pl.semaphore_wait(barrier, greeted)
-
-    def remote(src, dst, send_sem, recv_sem, which):
-        return pltpu.make_async_remote_copy(
-            src_ref=src, dst_ref=dst, send_sem=send_sem, recv_sem=recv_sem,
-            device_id=device(which), device_id_type=pl.DeviceIdType.MESH,
-        )
-
-    def piece(owner, part):
-        return coefs.at[owner, pl.ds(part * part_rows, part_rows)]
-
-    def ring(way, step):
-        back = -(step // 2) if way == 0 else step // 2
-        part = step % 2 if way == 0 else 1 - step % 2
-        ref = piece(2 * row_at(spot + back) + col, part)
-        return remote(ref, ref, ring_send.at[way, step], ring_recv.at[way, step], right if way == 0 else left)
-
-    def arrival(way, step):
-        back = -(step // 2) - 1 if way == 0 else step // 2 + 1
-        part = step % 2 if way == 0 else 1 - step % 2
-        ref = piece(2 * row_at(spot + back) + col, part)
-        return remote(ref, ref, ring_send.at[way, step], ring_recv.at[way, step], right if way == 0 else left)
-
-    def share(way, step, core):
-        back = -(step // 2) - 1 if way == 0 else step // 2 + 1
-        part = step % 2 if way == 0 else 1 - step % 2
-        ref = piece(2 * row_at(spot + back) + core, part)
-        return remote(ref, ref, pair_send.at[way, step], pair_recv.at[way, step], partner)
-
-    def share_own(core):
-        ref = coefs.at[2 * row + core]
-        return remote(ref, ref, pair_send.at[0, steps], pair_recv.at[0, steps], partner)
-
-    for step in range(2):
-        for way in range(2):
-            ring(way, step).start()
-    share_own(col).start()
-
     fetches[3].wait()
     for q in range(ints_ref.shape[1] // LANES):
         stage[q] = ints_ref[:, q * LANES:(q + 1) * LANES].astype(jnp.float32)
         for p in range(aux):
             lines = stage[q, pl.ds(p, tile, stride=aux), :]
             held[0, p * tile:(p + 1) * tile, q * LANES:(q + 1) * LANES] = lines.astype(held.dtype)
+
+    pl.semaphore_wait(barrier, greeted)
+
+    def remote(src, dst, send_sem, recv_sem, which):
+        return pltpu.make_async_remote_copy(
+            src_ref=src, dst_ref=dst, send_sem=send_sem, recv_sem=recv_sem,
+            device_id=device(which), device_id_type=pl.DeviceIdType.MESH,
+        )
+
+    def piece(owner, part):
+        return coefs.at[owner, pl.ds(part * part_rows, part_rows)]
+
+    def ring(way, step):
+        back = -(step // 2) if way == 0 else step // 2
+        part = step % 2 if way == 0 else 1 - step % 2
+        ref = piece(2 * row_at(spot + back) + col, part)
+        return remote(ref, ref, ring_send.at[way, step], ring_recv.at[way, step], right if way == 0 else left)
+
+    def arrival(way, step):
+        back = -(step // 2) - 1 if way == 0 else step // 2 + 1
+        part = step % 2 if way == 0 else 1 - step % 2
+        ref = piece(2 * row_at(spot + back) + col, part)
+        return remote(ref, ref, ring_send.at[way, step], ring_recv.at[way, step], right if way == 0 else left)
+
+    def share(way, step, core):
+        back = -(step // 2) - 1 if way == 0 else step // 2 + 1
+        part = step % 2 if way == 0 else 1 - step % 2
+        ref = piece(2 * row_at(spot + back) + core, part)
+        return remote(ref, ref, pair_send.at[way, step], pair_recv.at[way, step], partner)
+
+    def share_own(core):
+        ref = coefs.at[2 * row + core]
+        return remote(ref, ref, pair_send.at[0, steps], pair_recv.at[0, steps], partner)
+
+    for step in range(2):
+        for way in range(2):
+            ring(way, step).start()
+    share_own(col).start()
 
     back_copy = remote(held.at[0], held.at[2], int_send.at[0], int_recv.at[1], me - skip)
     next_copy = remote(held.at[0], held.at[1], int_send.at[1], int_recv.at[0], partner)
@@ -278,7 +278,7 @@
     def _():
         next_copy.wait_recv()
 
-    group = 2
+    group = 4
 
     def add_up(step, total):
         rows_of = pl.ds(pl.multiple_of(step * group * tile, group * tile), group * tile)

time: 45.3 us -> 44.7 us (0.987)
  Pallas kernels: 43.4 us -> 42.8 us
    pallas_call x1, Pallas kernels: 43.4 us -> 42.8 us  [ring_body(): pl.pallas_call(functools.partial(kernel, rows, aux, 1.0 / math.sqrt(aux *...]
where the time goes in v5:
time: 44.7 us; the launch traced here: 44.5 us
  Pallas kernels  42.8 us (96%)
  local copies, waits for them, and re-layouts  1.72 us (4%)
    pallas_call x1, Pallas kernels, ring_body(): pl.pallas_call(functools.partial(kernel, rows, aux, 1.0 / math.sqrt(aux *...  42.8 us
    unnamed x1, local copies, waits for them, and re-layouts  1.72 us

profile of v5, /device:TPU:1, one launch (start us, length us, event | category | flops | bytes accessed | tf_op | source)
XLA Modules:
  0.0 44.5 jit_solution(17884792719379364115)
XLA Ops:
  0.0 42.8 %shard_map.46 = f32[128,640]{1,0:T(8,128)} custom-call(bf16[1000,128]{1,0:T(8,128)(2,1)} %bitcast.6, bf16[1024,256]{1,0:T(8,128)(2,1)} %bitcast.5, s32[2,16]{1,0:T(2,128)} %bitcast.7, s32[1,16]{1,0:T(1,128)} %count_hbm.1), custom_call_target="tpu_custom_call" | custom-call | tf_op jit(solution)/shard_map/pallas_call | solution.py:389
  42.8 1.7 %copy.6 = f32[128,640]{1,0:T(8,128)} copy(f32[128,640]{1,0:T(8,128)} %shard_map.46) | data formatting | bytes 655360

commit v6 on v5

--- a/solution.py
+++ b/solution.py
@@ -134,6 +134,7 @@
     )
     coefs[me, whole:padded] = rest.astype(coefs.dtype)
     greeted = 3 + has_skip.astype(jnp.int32) + has_back.astype(jnp.int32) + has_cross.astype(jnp.int32)
+    out_ref[...] = jnp.zeros_like(out_ref)
     fetches[3].wait()
     for q in range(ints_ref.shape[1] // LANES):
         stage[q] = ints_ref[:, q * LANES:(q + 1) * LANES].astype(jnp.float32)
@@ -242,6 +243,15 @@
             if step + 2 < steps:
                 ring(way, step + 2).start()
             share(way, step, col).start()
+        if step == steps - 2:
+            @pl.when(has_skip)
+            def _():
+                remote(held.at[0], held.at[2], int_send.at[0], int_recv.at[1], me - skip).wait_recv()
+
+            @pl.when(jnp.logical_and(col == 0, has_skip))
+            def _():
+                pass_copy.start()
+
         if step == 3:
             @pl.when(is_via)
             def _():
@@ -262,14 +272,6 @@
     opposite = row_at(spot + depth)
     pick(2 * opposite + col)
 
-    @pl.when(has_skip)
-    def _():
-        remote(held.at[0], held.at[2], int_send.at[0], int_recv.at[1], me - skip).wait_recv()
-
-    @pl.when(jnp.logical_and(col == 0, has_skip))
-    def _():
-        pass_copy.start()
-
     for way in range(2):
         share(way, steps - 1, 1 - col).wait_recv()
     pick(2 * opposite + 1 - col)
@@ -299,7 +301,6 @@
     zero = jnp.zeros((tile, NEED * tile), jnp.float32)
     total = lax.fori_loop(0, aux // group, add_up, zero) * scale
     diag, above, far = (total[:, k * tile:(k + 1) * tile] for k in range(NEED))
-    out_ref[...] = jnp.zeros_like(out_ref)
     sent[0] = above.T
     sent[1] = far.T
     give_next = remote(sent.at[0], landed.at[0], res_send.at[0], res_recv.at[0], me + 1)

time: 44.7 us -> 44.2 us (0.989)
  Pallas kernels: 42.8 us -> 42.3 us
where the time goes in v6:
time: 44.2 us; the launch traced here: 44.1 us
  Pallas kernels  42.3 us (96%)
  local copies, waits for them, and re-layouts  1.72 us (4%)
    pallas_call x1, Pallas kernels, ring_body(): pl.pallas_call(functools.partial(kernel, rows, aux, 1.0 / math.sqrt(aux *...  42.3 us
    unnamed x1, local copies, waits for them, and re-layouts  1.72 us

profile of v6, /device:TPU:1, one launch (start us, length us, event | category | flops | bytes accessed | tf_op | source)
XLA Modules:
  0.0 44.1 jit_solution(6222398578457933214)
XLA Ops:
  0.0 42.3 %shard_map.46 = f32[128,640]{1,0:T(8,128)} custom-call(bf16[1000,128]{1,0:T(8,128)(2,1)} %bitcast.6, bf16[1024,256]{1,0:T(8,128)(2,1)} %bitcast.5, s32[2,16]{1,0:T(2,128)} %bitcast.7, s32[1,16]{1,0:T(1,128)} %count_hbm.1), custom_call_target="tpu_custom_call" | custom-call | tf_op jit(solution)/shard_map/pallas_call | solution.py:390
  42.4 1.7 %copy.6 = f32[128,640]{1,0:T(8,128)} copy(f32[128,640]{1,0:T(8,128)} %shard_map.46) | data formatting | bytes 655360
